TPU v7x, 32 devices: a whole 2x2x4 slice. The times are simulated.
32 devices in a mesh: parts: 2 (over y), pre: 4 (over z), tp: 4 (over x, core).
Axes of the slice: x: 2, y: 2, z: 4, core: 2. Of those that a mesh axis runs over, the one named last changes fastest.
Arguments:
- queries: bfloat16 [4096, 4096], P(('parts', 'pre'), 'tp'), parts along dimension 0, may hold values from -4.5 to 4.5
- new_keys: bfloat16 [4096, 1024], P(('parts', 'pre'), 'tp'), parts along dimension 0, may hold values from -4.5 to 4.5
- new_values: bfloat16 [4096, 1024], P(('parts', 'pre'), 'tp'), parts along dimension 0, may hold values from -4 to 4
- lengths: int32 [8], P('parts'), parts along dimension 0, may hold values from 1 to 1024, 2048 in all
- block_slot: int32 [256], P('parts'), parts along dimension 0, may hold values from 0 to 127, as said below
Outputs:
- attended: bfloat16 [4096, 4096], P(('parts', 'pre'), 'tp'), parts along dimension 0
- kv_cache: bfloat16 [256, 16, 2048], P(('parts', 'pre'), None, 'tp'), parts along dimension 0
There are 2 independent parts, one for each index of `parts`. A program takes and returns all parts, laid end to end along the dimension named above; each array names one. Nothing has to cross between parts.
Inputs may be any that keep to these rules, and one draw needn't show every extreme that they name: `block_slot`: A permutation of the 128 slots. The 32 blocks held by one index of pre (blocks of its own rows) take exactly 8 slots of every decode owner.
All inputs are finite; a program needn't handle non-finite values.
Results may differ from a plain program's by a relative error of at most 0.0036.
Values may be sent and summed in bfloat16 or wider, within the bound.
No kernel may reach another device: no remote copies, remote signals or barrier semaphores. Data moves between devices by JAX's collectives and lax.ppermute only.
A program may use at most 64 MiB of HBM per device.

v0:
```python
import functools
import math

import jax
import jax.numpy as jnp
from jax import lax
from jax.experimental import pallas as pl
from jax.experimental.pallas import tpu as pltpu
from jax.sharding import PartitionSpec as P

HD = 128
BLK = 16
GROUP = 4
TILE = 256
ONES = 16
MASKED = -1e30
EXP_SCALE = math.log2(math.e) * HD ** (-0.5)

VMEM = pl.BlockSpec(memory_space=pltpu.VMEM)
SMEM = pl.BlockSpec(memory_space=pltpu.SMEM)
HBM = pl.BlockSpec(memory_space=pltpu.HBM)


def start_of(lengths_ref, position):
    end = jnp.int32(0)
    start = jnp.int32(0)
    for r in range(lengths_ref.shape[0]):
        end = end + lengths_ref[r]
        start = jnp.where(end <= position, end, start)
    return start


def row_starts(lengths_ref, positions):
    end = jnp.int32(0)
    starts = jnp.zeros_like(positions)
    for r in range(lengths_ref.shape[0]):
        end = end + lengths_ref[r]
        starts = jnp.where(positions >= end, end, starts)
    return starts


def fill_bias(bias_ref, lengths_ref, row_first, key_first, low, high, causal):
    shape = (high - low, TILE)
    positions = row_first + lax.broadcasted_iota(jnp.int32, (8, TILE), 1)
    starts = row_starts(lengths_ref, positions)
    keys = key_first + low + lax.broadcasted_iota(jnp.int32, shape, 0)
    keys = keys.reshape((high - low) // 8, 8, TILE)
    allowed = keys >= starts[None]
    if causal:
        allowed = allowed & (keys <= positions[None])
    bias_ref[low:high] = jnp.where(allowed, 0.0, MASKED).reshape(shape)


def turn_values(v_ref, turned):
    for g in range(turned.shape[0]):
        turned[g, :HD] = v_ref[:, g * HD : (g + 1) * HD].T
        turned[g, HD:] = jnp.ones((ONES, turned.shape[2]), turned.dtype)


def lanes_of(tile, j):
    return slice((tile * GROUP + j) * TILE, (tile * GROUP + j + 1) * TILE)


def absorb(q_ref, k_ref, turned, bias_ref, old_state, tile, low, high, emit):
    for g in range(turned.shape[0]):
        keys = k_ref[low:high, g * HD : (g + 1) * HD]
        values = turned[g, :, low:high]
        heads = range(g * GROUP, (g + 1) * GROUP)
        queries = jnp.concatenate(
            [q_ref[tile * TILE : (tile + 1) * TILE, h * HD : (h + 1) * HD] for h in heads], axis=0
        )
        all_scores = lax.dot_general(
            keys, queries, (((1,), (1,)), ((), ())), preferred_element_type=jnp.float32
        )
        all_weights, tops, factors = [], [], []
        for j in range(GROUP):
            scores = all_scores[:, j * TILE : (j + 1) * TILE] + bias_ref[low:high]
            scores = scores.reshape((high - low) // 8, 8, TILE)
            highest = jnp.max(jnp.max(scores, axis=0), axis=0, keepdims=True)
            new = jnp.broadcast_to(highest, (8, TILE))
            if old_state is not None:
                old = old_state[1][g, :, lanes_of(tile, j)]
                new = jnp.maximum(old, new)
                factors.append(jnp.exp2((old - new) * EXP_SCALE))
            weights = jnp.exp2((scores - new[None]) * EXP_SCALE)
            all_weights.append(weights.reshape(high - low, TILE).astype(jnp.bfloat16))
            tops.append(new)
        all_added = jnp.dot(
            values, jnp.concatenate(all_weights, axis=1), preferred_element_type=jnp.float32
        )
        for j in range(GROUP):
            added = all_added[:, j * TILE : (j + 1) * TILE]
            value, total = added[:HD], added[HD : HD + 8]
            if old_state is not None:
                total = total + old_state[2][g, :, lanes_of(tile, j)] * factors[j]
                kept = old_state[0][g, :, lanes_of(tile, j)].reshape(HD // 8, 8, TILE)
                value = value + (kept * factors[j][None]).reshape(HD, TILE)
            emit(g, j, value, tops[j], total)


def keep(state, tile):
    def emit(g, j, value, top, total):
        for ref, array in zip(state, (value, top, total)):
            ref[g, :, lanes_of(tile, j)] = array

    return emit


def finish(out_ref, row):
    def emit(g, j, value, top, total):
        head = g * GROUP + j
        value = value.reshape(HD // 8, 8, TILE) * (1.0 / total)[None]
        value = value.reshape(HD, TILE).astype(out_ref.dtype).T
        out_ref[row : row + TILE, head * HD : (head + 1) * HD] = value

    return emit


def block_of(k_ref, v_ref, row):
    parts = []
    for g in range(k_ref.shape[1] // HD):
        span = slice(g * HD, (g + 1) * HD)
        parts += [k_ref[pl.ds(row, BLK), span], v_ref[pl.ds(row, BLK), span]]
    return jnp.concatenate(parts, axis=1)


def own_slot(slot, me, blocks):
    local = slot - me * blocks
    return jnp.where((local >= 0) & (local < blocks), local, blocks)


def own_kernel(
    pre, hops, lengths_ref, slot_ref, q_hbm, k_hbm, v_hbm,
    acc_ref, top_ref, sum_ref, sent_hbm,
    q_ref, k_ref, v_ref, turned, bias, sent, counts, sems,
):
    rows = q_ref.shape[0]
    blocks = rows // BLK
    per_peer = blocks // pre
    spare = sent.shape[0] - 1
    me = lax.axis_index("pre")
    first = me * rows
    loads = [
        pltpu.make_async_copy(src, dst, sems.at[n])
        for n, (src, dst) in enumerate(((k_hbm, k_ref), (v_hbm, v_ref), (q_hbm, q_ref)))
    ]
    for load in loads:
        load.start()
    for owner in range(pre):
        counts[owner] = 0
    loads[0].wait()
    loads[1].wait()

    def step(b, _):
        owner = slot_ref[me * blocks + b] // blocks
        n = counts[owner]
        counts[owner] = n + 1
        distance = lax.rem(owner - me + pre, pre)
        at = jnp.where(distance > hops, (distance - hops - 1) * per_peer + n, spare)
        sent[at] = block_of(k_ref, v_ref, pl.multiple_of(b * BLK, BLK))
        return 0

    lax.fori_loop(0, blocks, step, 0, unroll=4)
    store = pltpu.make_async_copy(sent.at[0:spare], sent_hbm, sems.at[3])
    store.start()
    turn_values(v_ref, turned)
    loads[2].wait()
    for tile in range(rows // TILE):
        high = (tile + 1) * TILE
        fill_bias(bias, lengths_ref, first + tile * TILE, first, 0, high, True)
        emit = keep((acc_ref, top_ref, sum_ref), tile)
        absorb(q_ref, k_ref, turned, bias, None, tile, 0, high, emit)
    store.wait()


def lowest_key(lengths_ref, hop, tile, rows):
    first = lax.axis_index("pre") * rows
    key_first = first - hop * rows
    low = jnp.maximum(start_of(lengths_ref, first + tile * TILE) - key_first, 0)
    return jnp.where(key_first >= 0, jnp.minimum(low, rows), rows)


def absorb_far(lengths_ref, hop, low, q_ref, k_ref, turned, bias, old_state, tile, emit):
    rows = q_ref.shape[0]
    first = lax.axis_index("pre") * rows
    for at in range(0, rows, TILE):

        @pl.when((low >= at) & (low < at + TILE))
        def _():
            fill_bias(
                bias, lengths_ref, first + tile * TILE, first - hop * rows, at, rows, False
            )
            absorb(q_ref, k_ref, turned, bias, old_state, tile, at, rows, emit)


def prev_kernel(
    lengths_ref, q_ref, k_ref, v_ref, acc_in, top_in, sum_in,
    out_hbm, acc_ref, top_ref, sum_ref, turned, bias, out_buf, sems,
):
    rows = q_ref.shape[0]
    old_state = (acc_in, top_in, sum_in)
    turn_values(v_ref, turned)
    stores = []
    for tile in range(rows // TILE):
        keep_it = keep((acc_ref, top_ref, sum_ref), tile)
        end_it = finish(out_buf, tile * TILE)

        def emit(*result):
            keep_it(*result)
            end_it(*result)

        low = lowest_key(lengths_ref, 1, tile, rows)
        absorb_far(lengths_ref, 1, low, q_ref, k_ref, turned, bias, old_state, tile, emit)

        @pl.when(low == rows)
        def _():
            for g in range(turned.shape[0]):
                for j in range(GROUP):
                    end_it(g, j, *(ref[g, :, lanes_of(tile, j)] for ref in old_state))

        at = slice(tile * TILE, (tile + 1) * TILE)
        stores.append(pltpu.make_async_copy(out_buf.at[at], out_hbm.at[at], sems.at[tile]))
        stores[-1].start()
    for store in stores:
        store.wait()


def far_kernel(
    hop, pre, last,
    lengths_ref, slot_ref, q_ref, k_ref, v_ref, acc_in, top_in, sum_in, cache_in, out_in,
    *refs,
):
    if last:
        out_hbm, cache_hbm, cache, turned, bias, out_buf, sems = refs
        state = None
    else:
        out_hbm, *state, turned, bias, out_buf, sems = refs
    rows = q_ref.shape[0]
    blocks = rows // BLK
    me = lax.axis_index("pre")
    old_state = (acc_in, top_in, sum_in)
    tiles = rows // TILE
    if last:
        source = lax.rem(me - hop + pre, pre)
        cache[...] = cache_in[...]

        def cache_step(b, _):
            at = own_slot(slot_ref[source * blocks + b], me, blocks)
            cache[at] = block_of(k_ref, v_ref, pl.multiple_of(b * BLK, BLK))
            return 0

        lax.fori_loop(0, blocks, cache_step, 0, unroll=4)
        cache_store = pltpu.make_async_copy(cache.at[0:blocks], cache_hbm, sems.at[tiles])
        cache_store.start()

    lows = [lowest_key(lengths_ref, hop, tile, rows) for tile in range(tiles)]
    stores = []

    @pl.when(lows[0] < rows)
    def _():
        turn_values(v_ref, turned)

    for tile, low in enumerate(lows):
        end_it = finish(out_buf, tile * TILE)

        def emit(*result):
            if not last:
                keep(state, tile)(*result)
            end_it(*result)

        at = slice(tile * TILE, (tile + 1) * TILE)
        stores.append(pltpu.make_async_copy(out_buf.at[at], out_hbm.at[at], sems.at[tile]))
        absorb_far(lengths_ref, hop, low, q_ref, k_ref, turned, bias, old_state, tile, emit)
        pl.when(low < rows)(stores[-1].start)
    for low, store in zip(lows, stores):
        pl.when(low < rows)(store.wait)
    if last:
        cache_store.wait()


def place_kernel(pre, hops, slot_ref, got_ref, *refs):
    near, cache_ref = refs[:-1], refs[-1]
    blocks = near[0].shape[0] // BLK
    per_peer = blocks // pre
    me = lax.axis_index("pre")
    for back in range(hops):
        k_ref, v_ref = near[2 * back], near[2 * back + 1]
        source = lax.rem(me - back + pre, pre)

        def near_step(b, _):
            at = own_slot(slot_ref[source * blocks + b], me, blocks)
            cache_ref[at] = block_of(k_ref, v_ref, pl.multiple_of(b * BLK, BLK))
            return 0

        lax.fori_loop(0, blocks, near_step, 0, unroll=4)
    for distance in range(hops + 1, pre):
        source = lax.rem(me - distance + pre, pre)

        def far_step(b, n):
            at = own_slot(slot_ref[source * blocks + b], me, blocks)
            cache_ref[at] = got_ref[(distance - hops - 1) * per_peer + jnp.minimum(n, per_peer - 1)]
            return n + jnp.where(at < blocks, 1, 0)

        lax.fori_loop(0, blocks, far_step, jnp.int32(0), unroll=4)


def on_device(queries, new_keys, new_values, lengths, block_slot):
    rows, q_width = queries.shape
    kv_width = new_keys.shape[1]
    kv_count = kv_width // HD
    blocks = rows // BLK
    pre = lax.axis_size("pre")
    per_peer = blocks // pre
    hops = pre // 2
    far = (pre - 1 - hops) * per_peer
    tiles = rows // TILE
    bf16, f32 = jnp.bfloat16, jnp.float32
    shape = jax.ShapeDtypeStruct
    params = pltpu.CompilerParams(vmem_limit_bytes=24 * 2**20)
    ring = [(i, (i + 1) % pre) for i in range(pre)]
    state = (
        shape((kv_count, HD, GROUP * rows), f32),
        shape((kv_count, 8, GROUP * rows), f32),
        shape((kv_count, 8, GROUP * rows), f32),
    )
    turned = pltpu.VMEM((kv_count, HD + ONES, rows), bf16)
    bias = pltpu.VMEM((rows, TILE), f32)
    out_buf = pltpu.VMEM((rows, q_width), bf16)
    attended_shape = shape(queries.shape, bf16)
    cache_shape = shape((blocks, BLK, 2 * kv_width), bf16)
    open_cache = (blocks + 1, BLK, 2 * kv_width)

    def cost(share, moved):
        pairs = int(rows * rows * share)
        return pl.CostEstimate(
            flops=4 * pairs * q_width,
            bytes_accessed=moved * 2**20,
            transcendentals=pairs * kv_count * GROUP,
        )

    pk = lax.ppermute(new_keys, "pre", ring)
    pv = lax.ppermute(new_values, "pre", ring)

    *running, sent = pl.pallas_call(
        functools.partial(own_kernel, pre, hops),
        out_shape=state + (shape((far, BLK, 2 * kv_width), bf16),),
        in_specs=[SMEM, SMEM, HBM, HBM, HBM],
        out_specs=(VMEM,) * 3 + (HBM,),
        scratch_shapes=[
            pltpu.VMEM((rows, q_width), bf16),
            pltpu.VMEM((rows, kv_width), bf16),
            pltpu.VMEM((rows, kv_width), bf16),
            turned,
            bias,
            pltpu.VMEM((far + 1, BLK, 2 * kv_width), bf16),
            pltpu.SMEM((pre,), jnp.int32),
            pltpu.SemaphoreType.DMA((4,)),
        ],
        cost_estimate=cost(1, 4),
        compiler_params=params,
        name="own_attention",
    )(lengths, block_slot, queries, new_keys, new_values)
    got = []
    for distance in range(hops + 1, pre):
        at = (distance - hops - 1) * per_peer
        pairs = [(i, (i + distance) % pre) for i in range(pre)]
        got.append(lax.ppermute(sent[at : at + per_peer], "pre", pairs))
    got = jnp.concatenate(got, axis=0)
    running[1], pk = lax.optimization_barrier((running[1], pk))
    running[2], pv = lax.optimization_barrier((running[2], pv))

    chain = [(new_keys, new_values), (pk, pv)]
    for hop in range(2, hops + 1):
        chain.append(tuple(lax.ppermute(piece, "pre", ring) for piece in chain[-1]))

    attended, *running = pl.pallas_call(
        prev_kernel,
        out_shape=(attended_shape,) + state,
        in_specs=[SMEM] + [VMEM] * 6,
        out_specs=(HBM,) + (VMEM,) * 3,
        scratch_shapes=[turned, bias, out_buf, pltpu.SemaphoreType.DMA((tiles,))],
        cost_estimate=cost(1, 5),
        compiler_params=params,
        name="prev_attention",
    )(lengths, queries, pk, pv, *running)

    flat = [piece for pair in chain[:-1] for piece in pair]
    cache = pl.pallas_call(
        functools.partial(place_kernel, pre, hops),
        out_shape=shape(open_cache, bf16),
        in_specs=[SMEM] + [VMEM] * (1 + len(flat)),
        out_specs=VMEM,
        cost_estimate=cost(0, 2),
        compiler_params=params,
        name="place_blocks",
    )(block_slot, got, *flat)
    for hop in range(2, hops + 1):
        last = hop == hops
        attended, *running = pl.pallas_call(
            functools.partial(far_kernel, hop, pre, last),
            out_shape=(attended_shape,) + ((cache_shape,) if last else state),
            in_specs=[SMEM, SMEM] + [VMEM] * 7 + [HBM],
            out_specs=(HBM,) + ((HBM,) if last else (VMEM,) * 3),
            scratch_shapes=([pltpu.VMEM(open_cache, bf16)] if last else [])
            + [turned, bias, out_buf, pltpu.SemaphoreType.DMA((tiles + 1,))],
            input_output_aliases={9: 0},
            cost_estimate=cost(0.25, 2),
            compiler_params=params,
            name="far_attention",
        )(lengths, block_slot, queries, *chain[hop], *running, cache, attended)
    return (attended, running[0])


def solution(mesh):
    placed = (
        P(("parts", "pre"), "tp"),
        P(("parts", "pre"), "tp"),
        P(("parts", "pre"), "tp"),
        P("parts"),
        P("parts"),
    )
    return jax.shard_map(
        on_device,
        mesh=mesh,
        in_specs=placed,
        out_specs=(P(("parts", "pre"), "tp"), P(("parts", "pre"), None, "tp")),
        check_vma=False,
    )
```

profile of v0, /device:TPU:13, one launch (start us, length us, event | category | flops | bytes accessed | tf_op | source)
XLA Modules:
  0.0 41.3 jit_solution(6724574932960268904)
XLA Ops:
  0.6 1.3 %collective-permute-start = (bf16[512,256]{1,0:T(8,128)(2,1)}, bf16[512,256]{1,0:T(8,128)(2,1)S(1)}, u32[]{:S(2)}, u32[]{:S(2)}) collective-permute-start(bf16[512,256]{1,0:T(8,128)(2,1)} %refs_0_.1), channel_id=1, source_target_pairs={{0,4},{4,8},{8,12},{12,0},{1,5},{5,9},{9,13},{13,1},{2,6},{6,10},{... | collective-permute-start | bytes 786440 | tf_op jit(solution)/shard_map/ppermute | solution.py:341
  2.0 1.3 %collective-permute-start.2 = (bf16[512,256]{1,0:T(8,128)(2,1)}, bf16[512,256]{1,0:T(8,128)(2,1)S(1)}, u32[]{:S(2)}, u32[]{:S(2)}) collective-permute-start(bf16[512,256]{1,0:T(8,128)(2,1)} %refs_1_.1), channel_id=1, source_target_pairs={{0,4},{4,8},{8,12},{12,0},{1,5},{5,9},{9,13},{13,1},{2,6},{6,10},{... | collective-permute-start | bytes 786440 | tf_op jit(solution)/shard_map/ppermute | solution.py:342
  3.3 0.0 copy-start
  3.3 1.2 %copy-done = bf16[512,1024]{1,0:T(8,128)(2,1)S(1)} copy-done((bf16[512,1024]{1,0:T(8,128)(2,1)S(1)}, bf16[512,1024]{1,0:T(8,128)(2,1)}, u32[]{:S(2)}) %copy-start) | copy-done | bytes 1048600
  4.5 0.0 copy-start.2
  4.5 0.9 %copy-done.2 = bf16[512,256]{1,0:T(8,128)(2,1)S(1)} copy-done((bf16[512,256]{1,0:T(8,128)(2,1)S(1)}, bf16[512,256]{1,0:T(8,128)(2,1)}, u32[]{:S(2)}) %copy-start.2) | copy-done | bytes 262168
  5.5 0.0 copy-start.4
  5.5 0.9 %copy-done.4 = bf16[512,256]{1,0:T(8,128)(2,1)S(1)} copy-done((bf16[512,256]{1,0:T(8,128)(2,1)S(1)}, bf16[512,256]{1,0:T(8,128)(2,1)}, u32[]{:S(2)}) %copy-start.4) | copy-done | bytes 262168
  6.4 0.0 copy-start.5
  6.4 0.7 %copy-done.5 = s32[128]{0:T(128)S(1)} copy-done((s32[128]{0:T(128)S(1)}, s32[128]{0:T(128)}, u32[]{:S(2)}) %copy-start.5) | copy-done | bytes 536
  7.1 0.0 copy-start.6
  7.1 0.7 %copy-done.6 = s32[4]{0:T(128)S(1)} copy-done((s32[4]{0:T(128)S(1)}, s32[4]{0:T(128)}, u32[]{:S(2)}) %copy-start.6) | copy-done | bytes 40
  7.7 0.0 copy-start.3
  7.7 0.0 copy-start.1
  7.7 4.1 %own_attention.1 = (f32[2,128,2048]{2,1,0:T(8,128)S(1)}, f32[2,8,2048]{2,1,0:T(8,128)S(1)}, f32[2,8,2048]{2,1,0:T(8,128)S(1)}, bf16[8,16,512]{2,1,0:T(8,128)(2,1)S(1)}) custom-call(s32[4]{0:T(128)S(1)} %copy-done.6, s32[128]{0:T(128)S(1)} %copy-done.5, bf16[512,1024]{1,0:T(8,128)(2,1)S(1)} %copy-done, bf16[512,256]{1,0:T(8,128)(2,1)S(1)} %copy-done.2, ...), custom_call_target="tpu_custom_call" | custom-call | flops 1073741824 | bytes 4194304 | tf_op jit(solution)/shard_map/own_attention/pallas_call | solution.py:344
  11.8 0.0 collective-permute-done.k_ref.refs_2_
  11.8 1.8 %collective-permute-done.2.v_ref.refs_3_ = bf16[512,256]{1,0:T(8,128)(2,1)S(1)} collective-permute-done((bf16[512,256]{1,0:T(8,128)(2,1)}, bf16[512,256]{1,0:T(8,128)(2,1)S(1)}, u32[]{:S(2)}, u32[]{:S(2)}) %collective-permute-start.2) | collective-permute-done | bytes 262176 | tf_op jit(solution)/shard_map/ppermute | solution.py:342
  13.7 1.3 %collective-permute-start.1 = (bf16[512,256]{1,0:T(8,128)(2,1)S(1)}, bf16[512,256]{1,0:T(8,128)(2,1)S(1)}, u32[]{:S(2)}, u32[]{:S(2)}) collective-permute-start(bf16[512,256]{1,0:T(8,128)(2,1)S(1)} %collective-permute-done.k_ref.refs_2_), channel_id=1, source_target_pairs={{0,4},{4,8},{8,12},{12,0},{1,5},{5,9},{9,13},{13,1},{2,6},{6,10},{... | collective-permute-start | bytes 786440 | tf_op jit(solution)/shard_map/ppermute | solution.py:374
  15.0 1.3 %collective-permute-start.3 = (bf16[512,256]{1,0:T(8,128)(2,1)S(1)}, bf16[512,256]{1,0:T(8,128)(2,1)S(1)}, u32[]{:S(2)}, u32[]{:S(2)}) collective-permute-start(bf16[512,256]{1,0:T(8,128)(2,1)S(1)} %collective-permute-done.2.v_ref.refs_3_), channel_id=1, source_target_pairs={{0,4},{4,8},{8,12},{12,0},{1,5},{5,9},{9,13},{13,1},{2,6},{6,10},{... | collective-permute-start | bytes 786440 | tf_op jit(solution)/shard_map/ppermute | solution.py:374
  16.3 0.2 collective-permute-start.4
  16.4 16.6 %collective-permute-done.4.got_ref = bf16[8,16,512]{2,1,0:T(8,128)(2,1)S(1)} collective-permute-done((bf16[8,16,512]{2,1,0:T(8,128)(2,1)S(1)}, bf16[8,16,512]{2,1,0:T(8,128)(2,1)S(1)}, u32[]{:S(2)}, u32[]{:S(2)}) %collective-permute-start.4) | collective-permute-done | bytes 131104 | tf_op jit(solution)/shard_map/ppermute | solution.py:367
  33.1 0.0 copy-done.3
  33.1 1.1 %place_blocks.1.cache_in = bf16[33,16,512]{2,1,0:T(8,128)(2,1)S(1)} custom-call(s32[128]{0:T(128)S(1)} %copy-done.5, bf16[8,16,512]{2,1,0:T(8,128)(2,1)S(1)} %collective-permute-done.4.got_ref, bf16[512,256]{1,0:T(8,128)(2,1)S(1)} %copy-done.3, bf16[512,256]{1,0:T(8,128)(2,1)S(1)} %copy-done.4, bf16[512,256]{1,0:T(8,128)(2,1)S(1)} %collective-permute-done.k_ref.refs_2_, ...), custom_call_target="tpu_custom_call" | custom-call | bytes 2097152 | tf_op jit(solution)/shard_map/place_blocks/pallas_call | solution.py:388
  34.2 0.0 copy-done.1
  34.2 5.4 %prev_attention.1 = (bf16[512,1024]{1,0:T(8,128)(2,1)}, f32[2,128,2048]{2,1,0:T(8,128)S(1)}, f32[2,8,2048]{2,1,0:T(8,128)S(1)}, f32[2,8,2048]{2,1,0:T(8,128)S(1)}) custom-call(s32[4]{0:T(128)S(1)} %copy-done.6, bf16[512,1024]{1,0:T(8,128)(2,1)S(1)} %copy-done.1, bf16[512,256]{1,0:T(8,128)(2,1)S(1)} %collective-permute-done.k_ref.refs_2_, ...), custom_call_target="tpu_custom_call" | custom-call | flops 1073741824 | bytes 5242880 | tf_op jit(solution)/shard_map/prev_attention/pallas_call | solution.py:376
  39.5 0.0 collective-permute-done.1.k_ref
  39.5 0.0 collective-permute-done.3.v_ref
  39.6 1.6 %far_attention.1 = (bf16[512,1024]{1,0:T(8,128)(2,1)}, bf16[32,16,512]{2,1,0:T(8,128)(2,1)}) custom-call(s32[4]{0:T(128)S(1)} %copy-done.6, s32[128]{0:T(128)S(1)} %copy-done.5, bf16[512,1024]{1,0:T(8,128)(2,1)S(1)} %copy-done.1, bf16[512,256]{1,0:T(8,128)(2,1)S(1)} %collective-permute-done.1.k_ref, ...), custom_call_target="tpu_custom_call", output_to_operand_aliasing={{0}: (9, {})} | custom-call | flops 268435456 | bytes 2097152 | tf_op jit(solution)/shard_map/far_attention/pallas_call | solution.py:399
Async XLA Ops:
  0.6 11.2 %collective-permute-start = (bf16[512,256]{1,0:T(8,128)(2,1)}, bf16[512,256]{1,0:T(8,128)(2,1)S(1)}, u32[]{:S(2)}, u32[]{:S(2)}) collective-permute-start(bf16[512,256]{1,0:T(8,128)(2,1)} %refs_0_.1), channel_id=1, source_target_pairs={{0,4},{4,8},{8,12},{12,0},{1,5},{5,9},{9,13},{13,1},{2,6},{6,10},{... | collective-permute-start | bytes 786440 | tf_op jit(solution)/shard_map/ppermute | solution.py:341
  2.0 11.7 %collective-permute-start.2 = (bf16[512,256]{1,0:T(8,128)(2,1)}, bf16[512,256]{1,0:T(8,128)(2,1)S(1)}, u32[]{:S(2)}, u32[]{:S(2)}) collective-permute-start(bf16[512,256]{1,0:T(8,128)(2,1)} %refs_1_.1), channel_id=1, source_target_pairs={{0,4},{4,8},{8,12},{12,0},{1,5},{5,9},{9,13},{13,1},{2,6},{6,10},{... | collective-permute-start | bytes 786440 | tf_op jit(solution)/shard_map/ppermute | solution.py:342
  3.3 1.2 %copy-start = (bf16[512,1024]{1,0:T(8,128)(2,1)S(1)}, bf16[512,1024]{1,0:T(8,128)(2,1)}, u32[]{:S(2)}) copy-start(bf16[512,1024]{1,0:T(8,128)(2,1)} %q_ref.3) | copy-start | bytes 3145732
  4.5 0.9 %copy-start.2 = (bf16[512,256]{1,0:T(8,128)(2,1)S(1)}, bf16[512,256]{1,0:T(8,128)(2,1)}, u32[]{:S(2)}) copy-start(bf16[512,256]{1,0:T(8,128)(2,1)} %refs_0_.1) | copy-start | bytes 786436
  5.5 0.9 %copy-start.4 = (bf16[512,256]{1,0:T(8,128)(2,1)S(1)}, bf16[512,256]{1,0:T(8,128)(2,1)}, u32[]{:S(2)}) copy-start(bf16[512,256]{1,0:T(8,128)(2,1)} %refs_1_.1) | copy-start | bytes 786436
  6.4 0.7 %copy-start.5 = (s32[128]{0:T(128)S(1)}, s32[128]{0:T(128)}, u32[]{:S(2)}) copy-start(s32[128]{0:T(128)} %slot_ref.5) | copy-start | bytes 1540
  7.1 0.7 %copy-start.6 = (s32[4]{0:T(128)S(1)}, s32[4]{0:T(128)}, u32[]{:S(2)}) copy-start(s32[4]{0:T(128)} %lengths_ref.5) | copy-start | bytes 52
  7.7 25.3 %copy-start.3 = (bf16[512,256]{1,0:T(8,128)(2,1)S(1)}, bf16[512,256]{1,0:T(8,128)(2,1)}, u32[]{:S(2)}) copy-start(bf16[512,256]{1,0:T(8,128)(2,1)} %refs_0_.1) | copy-start | bytes 786436
  7.7 26.4 %copy-start.1 = (bf16[512,1024]{1,0:T(8,128)(2,1)S(1)}, bf16[512,1024]{1,0:T(8,128)(2,1)}, u32[]{:S(2)}) copy-start(bf16[512,1024]{1,0:T(8,128)(2,1)} %q_ref.3) | copy-start | bytes 3145732
  13.7 25.8 %collective-permute-start.1 = (bf16[512,256]{1,0:T(8,128)(2,1)S(1)}, bf16[512,256]{1,0:T(8,128)(2,1)S(1)}, u32[]{:S(2)}, u32[]{:S(2)}) collective-permute-start(bf16[512,256]{1,0:T(8,128)(2,1)S(1)} %collective-permute-done.k_ref.refs_2_), channel_id=1, source_target_pairs={{0,4},{4,8},{8,12},{12,0},{1,5},{5,9},{9,13},{13,1},{2,6},{6,10},{... | collective-permute-start | bytes 786440 | tf_op jit(solution)/shard_map/ppermute | solution.py:374
  15.0 24.6 %collective-permute-start.3 = (bf16[512,256]{1,0:T(8,128)(2,1)S(1)}, bf16[512,256]{1,0:T(8,128)(2,1)S(1)}, u32[]{:S(2)}, u32[]{:S(2)}) collective-permute-start(bf16[512,256]{1,0:T(8,128)(2,1)S(1)} %collective-permute-done.2.v_ref.refs_3_), channel_id=1, source_target_pairs={{0,4},{4,8},{8,12},{12,0},{1,5},{5,9},{9,13},{13,1},{2,6},{6,10},{... | collective-permute-start | bytes 786440 | tf_op jit(solution)/shard_map/ppermute | solution.py:374
  16.3 16.8 %collective-permute-start.4 = (bf16[8,16,512]{2,1,0:T(8,128)(2,1)S(1)}, bf16[8,16,512]{2,1,0:T(8,128)(2,1)S(1)}, u32[]{:S(2)}, u32[]{:S(2)}) collective-permute-start(bf16[8,16,512]{2,1,0:T(8,128)(2,1)S(1)} %get-tuple-element.24), channel_id=1, source_target_pairs={{0,12},{4,0},{8,4},{12,8},{1,13},{5,1},{9,5},{13,9},{2,14},{6,2},{... | collective-permute-start | bytes 393224 | tf_op jit(solution)/shard_map/ppermute | solution.py:367
where the time goes:
time: 41.7 us; the launch traced here: 41.3 us
  waiting for transfers between devices  18.5 us (44%)
  Pallas kernels  12.1 us (29%)
  starting transfers between devices  5.41 us (13%)
  local copies, waits for them, and re-layouts  4.44 us (11%)
  between operations  0.86 us (2%)
    ppermute x1, waiting for transfers between devices, on_device(): got.append(lax.ppermute(sent[at:at + per_peer], 'pre', pairs))  16.6 us
    pallas_call x1, Pallas kernels, on_device(): pl.pallas_call(prev_kernel, out_shape=(attended_shape,) + state, in_specs...  5.36 us
    unnamed x14, local copies, waits for them, and re-layouts  4.44 us
    pallas_call x1, Pallas kernels, on_device(): pl.pallas_call(functools.partial(own_kernel, pre, hops), out_shape=state...  4.1 us
    ppermute x2, starting transfers between devices, on_device(): lax.ppermute(piece, 'pre', ring)  2.59 us
    ppermute x1, waiting for transfers between devices, on_device(): pv = lax.ppermute(new_values, 'pre', ring)  1.84 us
    pallas_call x1, Pallas kernels, on_device(): pl.pallas_call(functools.partial(far_kernel, hop, pre, last), out_shape=(...  1.58 us
    ppermute x1, starting transfers between devices, on_device(): pk = lax.ppermute(new_keys, 'pre', ring)  1.35 us
  transfers between devices with their start and end apart: 5, of which 2 were waited for; matrix products, arithmetic and copies ran while one was open for 0% of the time, Pallas kernels for 26%

commit v1 on v0

v1 whole, which is shorter than its diff:
```python
import functools
import math

import jax
import jax.numpy as jnp
from jax import lax
from jax.experimental import pallas as pl
from jax.experimental.pallas import tpu as pltpu
from jax.sharding import PartitionSpec as P

HD = 128
BLK = 16
GROUP = 4
TILE = 256
ONES = 16
MASKED = -1e30
EXP_SCALE = math.log2(math.e) * HD ** (-0.5)

VMEM = pl.BlockSpec(memory_space=pltpu.VMEM)
SMEM = pl.BlockSpec(memory_space=pltpu.SMEM)
HBM = pl.BlockSpec(memory_space=pltpu.HBM)


def start_of(lengths_ref, position):
    end = jnp.int32(0)
    start = jnp.int32(0)
    for r in range(lengths_ref.shape[0]):
        end = end + lengths_ref[r]
        start = jnp.where(end <= position, end, start)
    return start


def row_starts(lengths_ref, positions):
    end = jnp.int32(0)
    starts = jnp.zeros_like(positions)
    for r in range(lengths_ref.shape[0]):
        end = end + lengths_ref[r]
        starts = jnp.where(positions >= end, end, starts)
    return starts


def fill_bias(bias_ref, lengths_ref, row_first, key_first, low, high, causal):
    shape = (high - low, TILE)
    positions = row_first + lax.broadcasted_iota(jnp.int32, (8, TILE), 1)
    starts = row_starts(lengths_ref, positions)
    keys = key_first + low + lax.broadcasted_iota(jnp.int32, shape, 0)
    keys = keys.reshape((high - low) // 8, 8, TILE)
    allowed = keys >= starts[None]
    if causal:
        allowed = allowed & (keys <= positions[None])
    bias_ref[low:high] = jnp.where(allowed, 0.0, MASKED).reshape(shape)


def turn_values(v_ref, turned):
    for g in range(turned.shape[0]):
        turned[g, :HD] = v_ref[:, g * HD : (g + 1) * HD].T
        turned[g, HD:] = jnp.ones((ONES, turned.shape[2]), turned.dtype)


def lanes_of(tile, j):
    return slice((tile * GROUP + j) * TILE, (tile * GROUP + j + 1) * TILE)


def weigh(q_ref, k_ref, bias_ref, old_top, tile, low, high, g, emit):
    keys = k_ref[low:high, g * HD : (g + 1) * HD]
    heads = range(g * GROUP, (g + 1) * GROUP)
    queries = jnp.concatenate(
        [q_ref[tile * TILE : (tile + 1) * TILE, h * HD : (h + 1) * HD] for h in heads], axis=0
    )
    all_scores = lax.dot_general(
        keys, queries, (((1,), (1,)), ((), ())), preferred_element_type=jnp.float32
    )
    for j in range(GROUP):
        scores = all_scores[:, j * TILE : (j + 1) * TILE] + bias_ref[low:high]
        scores = scores.reshape((high - low) // 8, 8, TILE)
        highest = jnp.max(jnp.max(scores, axis=0), axis=0, keepdims=True)
        top = jnp.broadcast_to(highest, (8, TILE))
        factor = None
        if old_top is not None:
            old = old_top[g, :, lanes_of(tile, j)]
            top = jnp.maximum(old, top)
            factor = jnp.exp2((old - top) * EXP_SCALE)
        weights = jnp.exp2((scores - top[None]) * EXP_SCALE)
        emit(j, weights.reshape(high - low, TILE).astype(jnp.bfloat16), top, factor)


def mix(values, weights, g, tile, old, emit):
    all_added = jnp.dot(values, weights, preferred_element_type=jnp.float32)
    for j in range(GROUP):
        at = lanes_of(tile, j)
        added = all_added[:, j * TILE : (j + 1) * TILE]
        value, total = added[:HD], added[HD : HD + 8]
        if old is not None:
            acc_ref, sum_ref, factor_ref = old
            factor = factor_ref[g, :, at]
            total = total + sum_ref[g, :, at] * factor
            kept = acc_ref[g, :, at].reshape(HD // 8, 8, TILE) * factor[None]
            value = value + kept.reshape(HD, TILE)
        emit(g, j, value, total)


def keep(state, tile):
    def emit(g, j, value, total):
        for ref, array in zip(state, (value, total)):
            ref[g, :, lanes_of(tile, j)] = array

    return emit


def finish(out_ref, row):
    def emit(g, j, value, total):
        head = g * GROUP + j
        value = value.reshape(HD // 8, 8, TILE) * (1.0 / total)[None]
        value = value.reshape(HD, TILE).astype(out_ref.dtype).T
        out_ref[row : row + TILE, head * HD : (head + 1) * HD] = value

    return emit


def block_of(k_ref, v_ref, row):
    parts = []
    for g in range(k_ref.shape[1] // HD):
        span = slice(g * HD, (g + 1) * HD)
        parts += [k_ref[pl.ds(row, BLK), span], v_ref[pl.ds(row, BLK), span]]
    return jnp.concatenate(parts, axis=1)


def own_slot(slot, me, blocks):
    local = slot - me * blocks
    return jnp.where((local >= 0) & (local < blocks), local, blocks)


def own_kernel(
    pre, hops, lengths_ref, slot_ref, q_hbm, k_hbm, v_hbm,
    acc_ref, sum_ref, top_ref, sent_hbm,
    q_ref, k_ref, v_ref, turned, bias, sent, counts, sems,
):
    rows = q_ref.shape[0]
    blocks = rows // BLK
    per_peer = blocks // pre
    spare = sent.shape[0] - 1
    me = lax.axis_index("pre")
    first = me * rows
    loads = [
        pltpu.make_async_copy(src, dst, sems.at[n])
        for n, (src, dst) in enumerate(((k_hbm, k_ref), (v_hbm, v_ref), (q_hbm, q_ref)))
    ]
    for load in loads:
        load.start()
    for owner in range(pre):
        counts[owner] = 0
    loads[0].wait()
    loads[1].wait()

    def step(b, _):
        owner = slot_ref[me * blocks + b] // blocks
        n = counts[owner]
        counts[owner] = n + 1
        distance = lax.rem(owner - me + pre, pre)
        at = jnp.where(distance > hops, (distance - hops - 1) * per_peer + n, spare)
        sent[at] = block_of(k_ref, v_ref, pl.multiple_of(b * BLK, BLK))
        return 0

    lax.fori_loop(0, blocks, step, 0, unroll=4)
    store = pltpu.make_async_copy(sent.at[0:spare], sent_hbm, sems.at[3])
    store.start()
    turn_values(v_ref, turned)
    loads[2].wait()
    for tile in range(rows // TILE):
        high = (tile + 1) * TILE
        fill_bias(bias, lengths_ref, first + tile * TILE, first, 0, high, True)
        for g in range(turned.shape[0]):
            all_weights = []

            def emit(j, weights, top, factor):
                all_weights.append(weights)
                top_ref[g, :, lanes_of(tile, j)] = top

            weigh(q_ref, k_ref, bias, None, tile, 0, high, g, emit)
            all_weights = jnp.concatenate(all_weights, axis=1)
            mix(turned[g, :, :high], all_weights, g, tile, None, keep((acc_ref, sum_ref), tile))
    store.wait()


def lowest_key(lengths_ref, hop, tile, rows):
    first = lax.axis_index("pre") * rows
    key_first = first - hop * rows
    low = jnp.maximum(start_of(lengths_ref, first + tile * TILE) - key_first, 0)
    return jnp.where(key_first >= 0, jnp.minimum(low, rows), rows)


def where_seen(low, rows, act):
    for at in range(0, rows, TILE):
        pl.when((low >= at) & (low < at + TILE))(functools.partial(act, at))


def scores_kernel(hop, lengths_ref, q_ref, k_ref, old_top, weights_ref, factor_ref, top_ref, bias):
    rows = q_ref.shape[0]
    first = lax.axis_index("pre") * rows
    for tile in range(rows // TILE):

        def act(at):
            fill_bias(
                bias, lengths_ref, first + tile * TILE, first - hop * rows, at, rows, False
            )
            for g in range(weights_ref.shape[1]):

                def emit(j, weights, top, factor):
                    weights_ref[tile, g, at:rows, j * TILE : (j + 1) * TILE] = weights
                    top_ref[g, :, lanes_of(tile, j)] = top
                    factor_ref[g, :, lanes_of(tile, j)] = factor

                weigh(q_ref, k_ref, bias, old_top, tile, at, rows, g, emit)

        where_seen(lowest_key(lengths_ref, hop, tile, rows), rows, act)


def values_kernel(
    hop, first_out, last, lengths_ref, v_ref, weights_ref, factor_ref, acc_in, sum_in, *refs
):
    refs = refs if first_out else refs[1:]
    out_hbm, *state, turned, out_buf, sems = refs
    rows = v_ref.shape[0]
    tiles = rows // TILE
    kv_count = turned.shape[0]
    lows = [lowest_key(lengths_ref, hop, tile, rows) for tile in range(tiles)]
    pl.when(lows[0] < rows)(functools.partial(turn_values, v_ref, turned))
    stores = []
    for tile, low in enumerate(lows):
        end_it = finish(out_buf, tile * TILE)

        def act(at):
            def emit(*result):
                if not last:
                    keep(state, tile)(*result)
                end_it(*result)

            for g in range(kv_count):
                weights = weights_ref[tile, g, at:rows]
                old = (acc_in, sum_in, factor_ref)
                mix(turned[g, :, at:rows], weights, g, tile, old, emit)

        where_seen(low, rows, act)
        span = slice(tile * TILE, (tile + 1) * TILE)
        store = pltpu.make_async_copy(out_buf.at[span], out_hbm.at[span], sems.at[tile])
        stores.append(store)
        if first_out:

            @pl.when(low == rows)
            def _():
                for g in range(kv_count):
                    for j in range(GROUP):
                        end_it(g, j, *(ref[g, :, lanes_of(tile, j)] for ref in (acc_in, sum_in)))

            store.start()
        else:
            pl.when(low < rows)(store.start)
    for low, store in zip(lows, stores):
        if first_out:
            store.wait()
        else:
            pl.when(low < rows)(store.wait)


def place_kernel(pre, hops, slot_ref, got_ref, *refs):
    near, cache_hbm, cache, sem = refs[:-3], *refs[-3:]
    blocks = near[0].shape[0] // BLK
    per_peer = blocks // pre
    me = lax.axis_index("pre")
    for back in range(hops + 1):
        k_ref, v_ref = near[2 * back], near[2 * back + 1]
        source = lax.rem(me - back + pre, pre)

        def near_step(b, _):
            at = own_slot(slot_ref[source * blocks + b], me, blocks)
            cache[at] = block_of(k_ref, v_ref, pl.multiple_of(b * BLK, BLK))
            return 0

        lax.fori_loop(0, blocks, near_step, 0, unroll=4)
    for distance in range(hops + 1, pre):
        source = lax.rem(me - distance + pre, pre)

        def far_step(b, n):
            at = own_slot(slot_ref[source * blocks + b], me, blocks)
            cache[at] = got_ref[(distance - hops - 1) * per_peer + jnp.minimum(n, per_peer - 1)]
            return n + jnp.where(at < blocks, 1, 0)

        lax.fori_loop(0, blocks, far_step, jnp.int32(0), unroll=4)
    store = pltpu.make_async_copy(cache.at[0:blocks], cache_hbm, sem)
    store.start()
    store.wait()


def on_device(queries, new_keys, new_values, lengths, block_slot):
    rows, q_width = queries.shape
    kv_width = new_keys.shape[1]
    kv_count = kv_width // HD
    blocks = rows // BLK
    pre = lax.axis_size("pre")
    per_peer = blocks // pre
    hops = pre // 2
    far = (pre - 1 - hops) * per_peer
    tiles = rows // TILE
    bf16, f32 = jnp.bfloat16, jnp.float32
    shape = jax.ShapeDtypeStruct
    params = pltpu.CompilerParams(vmem_limit_bytes=24 * 2**20)
    all_params = pltpu.CompilerParams(vmem_limit_bytes=56 * 2**20)
    ring = [(i, (i + 1) % pre) for i in range(pre)]
    acc_shape = shape((kv_count, HD, GROUP * rows), f32)
    stat_shape = shape((kv_count, 8, GROUP * rows), f32)
    weights_shape = shape((tiles, kv_count, rows, GROUP * TILE), bf16)
    attended_shape = shape(queries.shape, bf16)
    cache_shape = shape((blocks, BLK, 2 * kv_width), bf16)
    turned = pltpu.VMEM((kv_count, HD + ONES, rows), bf16)
    bias = pltpu.VMEM((rows, TILE), f32)

    def cost(share, moved):
        pairs = int(rows * rows * share)
        return pl.CostEstimate(
            flops=4 * pairs * q_width,
            bytes_accessed=moved * 2**20,
            transcendentals=pairs * kv_count * GROUP,
        )

    def after(array, *others):
        return lax.optimization_barrier((array, *others))[0]

    k, v = lax.ppermute(new_keys, "pre", ring), lax.ppermute(new_values, "pre", ring)

    acc, total, top, sent = pl.pallas_call(
        functools.partial(own_kernel, pre, hops),
        out_shape=(acc_shape, stat_shape, stat_shape, shape((far, BLK, 2 * kv_width), bf16)),
        in_specs=[SMEM, SMEM, HBM, HBM, HBM],
        out_specs=(VMEM,) * 3 + (HBM,),
        scratch_shapes=[
            pltpu.VMEM((rows, q_width), bf16),
            pltpu.VMEM((rows, kv_width), bf16),
            pltpu.VMEM((rows, kv_width), bf16),
            turned,
            bias,
            pltpu.VMEM((far + 1, BLK, 2 * kv_width), bf16),
            pltpu.SMEM((pre,), jnp.int32),
            pltpu.SemaphoreType.DMA((4,)),
        ],
        cost_estimate=cost(1, 4),
        compiler_params=all_params,
        name="own_attention",
    )(lengths, block_slot, queries, new_keys, new_values)

    k = after(k, top)
    chain = [new_keys, new_values]
    attended = None
    for hop in range(1, hops + 1):
        first_out, last = hop == 1, hop == hops
        next_k = None if last else lax.ppermute(k, "pre", ring)
        weights, factor, top = pl.pallas_call(
            functools.partial(scores_kernel, hop),
            out_shape=(weights_shape, stat_shape, stat_shape),
            in_specs=[SMEM] + [VMEM] * 3,
            out_specs=(VMEM,) * 3,
            scratch_shapes=[bias],
            cost_estimate=cost(0.5, 3),
            compiler_params=params,
            name="scores",
        )(lengths, queries, k, top)
        v = after(v, factor)
        chain += [k, v]
        next_v = None if last else lax.ppermute(v, "pre", ring)
        attended, *state = pl.pallas_call(
            functools.partial(values_kernel, hop, first_out, last),
            out_shape=(attended_shape,) + (() if last else (acc_shape, stat_shape)),
            in_specs=[SMEM] + [VMEM] * 5 + ([] if first_out else [HBM]),
            out_specs=(HBM,) + (() if last else (VMEM, VMEM)),
            scratch_shapes=[
                turned,
                pltpu.VMEM((rows, q_width), bf16),
                pltpu.SemaphoreType.DMA((tiles,)),
            ],
            input_output_aliases={} if first_out else {6: 0},
            cost_estimate=cost(0.5, 3),
            compiler_params=params,
            name="values",
        )(lengths, v, weights, factor, acc, total, *([] if first_out else [attended]))
        if first_out:
            sent = after(sent, state[1] if state else attended)
            got = []
            for distance in range(hops + 1, pre):
                at = (distance - hops - 1) * per_peer
                pairs = [(i, (i + distance) % pre) for i in range(pre)]
                got.append(lax.ppermute(sent[at : at + per_peer], "pre", pairs))
            got = jnp.concatenate(got, axis=0)
        if not last:
            acc, total = state
            k, v = after(next_k, total), next_v

    cache = pl.pallas_call(
        functools.partial(place_kernel, pre, hops),
        out_shape=cache_shape,
        in_specs=[SMEM] + [VMEM] * (1 + len(chain)),
        out_specs=HBM,
        scratch_shapes=[
            pltpu.VMEM((blocks + 1, BLK, 2 * kv_width), bf16),
            pltpu.SemaphoreType.DMA,
        ],
        cost_estimate=cost(0, 2),
        compiler_params=params,
        name="place_blocks",
    )(block_slot, got, *chain)
    return (attended, cache)


def solution(mesh):
    placed = (
        P(("parts", "pre"), "tp"),
        P(("parts", "pre"), "tp"),
        P(("parts", "pre"), "tp"),
        P("parts"),
        P("parts"),
    )
    return jax.shard_map(
        on_device,
        mesh=mesh,
        in_specs=placed,
        out_specs=(P(("parts", "pre"), "tp"), P(("parts", "pre"), None, "tp")),
        check_vma=False,
    )
```

time: 41.7 us -> 34.4 us (0.82)
  the two profiles are of different devices: /device:TPU:13 before, /device:TPU:0 now
where the time goes in v1:
time: 34.4 us; the launch traced here: 34.2 us
  Pallas kernels  12.8 us (37%)
  starting transfers between devices  10.2 us (30%)
  local copies, waits for them, and re-layouts  5.3 us (15%)
  waiting for transfers between devices  5.03 us (15%)
  between operations  0.85 us (2%)
    pallas_call x1, Pallas kernels, on_device(): pl.pallas_call(functools.partial(own_kernel, pre, hops), out_shape=(acc_s...  6.31 us
    unnamed x20, local copies, waits for them, and re-layouts  5.3 us
    ppermute x1, starting transfers between devices, on_device(): got.append(lax.ppermute(sent[at:at + per_peer], 'pre', pairs))  3.19 us
    ppermute x1, starting transfers between devices, on_device(): lax.ppermute(new_keys, 'pre', ring)  3.08 us
    pallas_call x2, Pallas kernels, on_device(): pl.pallas_call(functools.partial(values_kernel, hop, first_out, last), ou...  2.43 us
    ppermute x1, starting transfers between devices, on_device(): next_v = None if last else lax.ppermute(v, 'pre', ring)  2.14 us
    pallas_call x1, Pallas kernels, on_device(): pl.pallas_call(functools.partial(place_kernel, pre, hops), out_shape=cach...  2.08 us
    ppermute x1, waiting for transfers between devices, on_device(): lax.ppermute(new_values, 'pre', ring)  2.07 us
  transfers between devices with their start and end apart: 5, of which 4 were waited for; matrix products, arithmetic and copies ran while one was open for 0% of the time, Pallas kernels for 31%

profile of v1, /device:TPU:0, one launch (start us, length us, event | category | flops | bytes accessed | tf_op | source)
XLA Modules:
  0.0 34.2 jit_solution(3631039343915120818)
XLA Ops:
  0.6 3.1 %collective-permute-start.1 = (bf16[512,256]{1,0:T(8,128)(2,1)}, bf16[512,256]{1,0:T(8,128)(2,1)S(1)}, u32[]{:S(2)}, u32[]{:S(2)}) collective-permute-start(bf16[512,256]{1,0:T(8,128)(2,1)} %refs_0_.1), channel_id=1, source_target_pairs={{0,4},{4,8},{8,12},{12,0},{1,5},{5,9},{9,13},{13,1},{2,6},{6,10},{... | collective-permute-start | bytes 786440 | tf_op jit(solution)/shard_map/ppermute | solution.py:328
  3.7 1.6 %collective-permute-start = (bf16[512,256]{1,0:T(8,128)(2,1)}, bf16[512,256]{1,0:T(8,128)(2,1)S(1)}, u32[]{:S(2)}, u32[]{:S(2)}) collective-permute-start(bf16[512,256]{1,0:T(8,128)(2,1)} %refs_1_.1), channel_id=1, source_target_pairs={{0,4},{4,8},{8,12},{12,0},{1,5},{5,9},{9,13},{13,1},{2,6},{6,10},{... | collective-permute-start | bytes 786440 | tf_op jit(solution)/shard_map/ppermute | solution.py:328
  5.3 6.3 %own_attention.1 = (f32[2,128,2048]{2,1,0:T(8,128)}, f32[2,8,2048]{2,1,0:T(8,128)}, f32[2,8,2048]{2,1,0:T(8,128)}, bf16[8,16,512]{2,1,0:T(8,128)(2,1)}) custom-call(s32[4]{0:T(128)} %lengths_ref.9, s32[128]{0:T(128)} %slot_ref.3, bf16[512,1024]{1,0:T(8,128)(2,1)} %q_ref.3, bf16[512,256]{1,0:T(8,128)(2,1)} %refs_0_.1, bf16[512,256]{1,0:T(8,128)(2,1)} %refs_1_.1), custom_call_target="tpu_custom_call" | custom-call | flops 1073741824 | bytes 4194304 | tf_op jit(solution)/shard_map/own_attention/pallas_call | solution.py:330
  11.6 1.5 %collective-permute-done.1.k_ref.refs_2_ = bf16[512,256]{1,0:T(8,128)(2,1)S(1)} collective-permute-done((bf16[512,256]{1,0:T(8,128)(2,1)}, bf16[512,256]{1,0:T(8,128)(2,1)S(1)}, u32[]{:S(2)}, u32[]{:S(2)}) %collective-permute-start.1) | collective-permute-done | bytes 262176 | tf_op jit(solution)/shard_map/ppermute | solution.py:328
  13.1 0.2 collective-permute-start.3
  13.2 0.0 copy-start.4
  13.2 0.7 %copy-done.4 = s32[4]{0:T(128)S(1)} copy-done((s32[4]{0:T(128)S(1)}, s32[4]{0:T(128)}, u32[]{:S(2)}) %copy-start.4) | copy-done | bytes 40
  13.9 0.0 copy-start.6
  13.9 1.2 %copy-done.6 = bf16[512,1024]{1,0:T(8,128)(2,1)S(1)} copy-done((bf16[512,1024]{1,0:T(8,128)(2,1)S(1)}, bf16[512,1024]{1,0:T(8,128)(2,1)}, u32[]{:S(2)}) %copy-start.6) | copy-done | bytes 1048600
  15.1 0.0 copy-start.8
  15.1 0.9 %copy-done.8 = f32[2,8,2048]{2,1,0:T(8,128)S(1)} copy-done((f32[2,8,2048]{2,1,0:T(8,128)S(1)}, f32[2,8,2048]{2,1,0:T(8,128)}, u32[]{:S(2)}) %copy-start.8) | copy-done | bytes 131096
  16.0 0.0 copy-start.9
  16.0 0.0 copy-start.7
  16.0 0.6 %scores.2 = (bf16[2,2,512,1024]{3,2,1,0:T(8,128)(2,1)S(1)}, f32[2,8,2048]{2,1,0:T(8,128)S(1)}, f32[2,8,2048]{2,1,0:T(8,128)S(1)}) custom-call(s32[4]{0:T(128)S(1)} %copy-done.4, bf16[512,1024]{1,0:T(8,128)(2,1)S(1)} %copy-done.6, bf16[512,256]{1,0:T(8,128)(2,1)S(1)} %collective-permute-done.1.k_ref.refs_2_, f32[2,8,2048]{2,1,0:T(8,128)S(1)} %copy-done.8), custom_call_target="tpu_custom_call" | custom-call | flops 536870912 | bytes 3145728 | tf_op jit(solution)/shard_map/scores/pallas_call | solution.py:356
  16.6 2.1 %collective-permute-done.v_ref.refs_3_ = bf16[512,256]{1,0:T(8,128)(2,1)S(1)} collective-permute-done((bf16[512,256]{1,0:T(8,128)(2,1)}, bf16[512,256]{1,0:T(8,128)(2,1)S(1)}, u32[]{:S(2)}, u32[]{:S(2)}) %collective-permute-start) | collective-permute-done | bytes 262176 | tf_op jit(solution)/shard_map/ppermute | solution.py:328
  18.7 2.1 %collective-permute-start.2 = (bf16[512,256]{1,0:T(8,128)(2,1)S(1)}, bf16[512,256]{1,0:T(8,128)(2,1)S(1)}, u32[]{:S(2)}, u32[]{:S(2)}) collective-permute-start(bf16[512,256]{1,0:T(8,128)(2,1)S(1)} %collective-permute-done.v_ref.refs_3_), channel_id=1, source_target_pairs={{0,4},{4,8},{8,12},{12,0},{1,5},{5,9},{9,13},{13,1},{2,6},{6,10},{... | collective-permute-start | bytes 786440 | tf_op jit(solution)/shard_map/ppermute | solution.py:368
  20.8 0.0 copy-start
  20.8 1.6 %copy-done = f32[2,128,2048]{2,1,0:T(8,128)S(1)} copy-done((f32[2,128,2048]{2,1,0:T(8,128)S(1)}, f32[2,128,2048]{2,1,0:T(8,128)}, u32[]{:S(2)}) %copy-start) | copy-done | bytes 2097176
  22.4 0.9 %copy-done.3 = f32[2,8,2048]{2,1,0:T(8,128)S(1)} copy-done((f32[2,8,2048]{2,1,0:T(8,128)S(1)}, f32[2,8,2048]{2,1,0:T(8,128)}, u32[]{:S(2)}) %copy-start.3) | copy-done | bytes 131096
  23.3 1.8 %values.2 = (bf16[512,1024]{1,0:T(8,128)(2,1)}, f32[2,128,2048]{2,1,0:T(8,128)S(1)}, f32[2,8,2048]{2,1,0:T(8,128)S(1)}) custom-call(s32[4]{0:T(128)S(1)} %copy-done.4, bf16[512,256]{1,0:T(8,128)(2,1)S(1)} %collective-permute-done.v_ref.refs_3_, bf16[2,2,512,1024]{3,2,1,0:T(8,128)(2,1)S(1)} %get-tuple-element.23.weights_ref, ...), custom_call_target="tpu_custom_call" | custom-call | flops 536870912 | bytes 3145728 | tf_op jit(solution)/shard_map/values/pallas_call | solution.py:369
  25.2 0.0 copy-done.9
  25.2 3.2 %collective-permute-start.4 = (bf16[8,16,512]{2,1,0:T(8,128)(2,1)S(1)}, bf16[8,16,512]{2,1,0:T(8,128)(2,1)S(1)}, u32[]{:S(2)}, u32[]{:S(2)}) collective-permute-start(bf16[8,16,512]{2,1,0:T(8,128)(2,1)S(1)} %copy-done.9), channel_id=1, source_target_pairs={{0,12},{4,0},{8,4},{12,8},{1,13},{5,1},{9,5},{13,9},{2,14},{6,2},{... | collective-permute-start | bytes 393224 | tf_op jit(solution)/shard_map/ppermute | solution.py:390
  28.4 0.0 collective-permute-done.3.k_ref.refs_4_
  28.4 0.0 copy-done.7
  28.4 1.4 %scores.3 = (bf16[2,2,512,1024]{3,2,1,0:T(8,128)(2,1)S(1)}, f32[2,8,2048]{2,1,0:T(8,128)S(1)}, f32[2,8,2048]{2,1,0:T(8,128)}) custom-call(s32[4]{0:T(128)S(1)} %copy-done.4, bf16[512,1024]{1,0:T(8,128)(2,1)S(1)} %copy-done.7, bf16[512,256]{1,0:T(8,128)(2,1)S(1)} %collective-permute-done.3.k_ref.refs_4_, f32[2,8,2048]{2,1,0:T(8,128)S(1)} %get-tuple-element.28.old_top), custom_call_target="tpu_custom_call" | custom-call | flops 536870912 | bytes 3145728 | tf_op jit(solution)/shard_map/scores/pallas_call | solution.py:356
  29.8 0.1 collective-permute-done.2.v_ref.refs_5_
  29.9 0.6 %values.3 = bf16[512,1024]{1,0:T(8,128)(2,1)} custom-call(s32[4]{0:T(128)S(1)} %copy-done.4, bf16[512,256]{1,0:T(8,128)(2,1)S(1)} %collective-permute-done.2.v_ref.refs_5_, bf16[2,2,512,1024]{3,2,1,0:T(8,128)(2,1)S(1)} %get-tuple-element.31.weights_ref, f32[2,8,2048]{2,1,0:T(8,128)S(1)} %get-tuple-element.29.factor_ref, ...), custom_call_target="tpu_custom_call", output_to_operand_aliasing={{}: (6, {})} | custom-call | flops 536870912 | bytes 3145728 | tf_op jit(solution)/shard_map/values/pallas_call | solution.py:369
  30.5 1.4 %collective-permute-done.4.got_ref = bf16[8,16,512]{2,1,0:T(8,128)(2,1)S(1)} collective-permute-done((bf16[8,16,512]{2,1,0:T(8,128)(2,1)S(1)}, bf16[8,16,512]{2,1,0:T(8,128)(2,1)S(1)}, u32[]{:S(2)}, u32[]{:S(2)}) %collective-permute-start.4) | collective-permute-done | bytes 131104 | tf_op jit(solution)/shard_map/ppermute | solution.py:390
  31.9 0.0 copy-done.1
  31.9 0.0 copy-done.2
  31.9 0.0 copy-done.5
  31.9 2.1 %place_blocks.1 = bf16[32,16,512]{2,1,0:T(8,128)(2,1)} custom-call(s32[128]{0:T(128)S(1)} %copy-done.5, bf16[8,16,512]{2,1,0:T(8,128)(2,1)S(1)} %collective-permute-done.4.got_ref, bf16[512,256]{1,0:T(8,128)(2,1)S(1)} %copy-done.2, bf16[512,256]{1,0:T(8,128)(2,1)S(1)} %copy-done.1, bf16[512,256]{1,0:T(8,128)(2,1)S(1)} %collective-permute-done.1.k_ref.refs_2_, ...), custom_call_target="tpu_custom_call" | custom-call | bytes 2097152 | tf_op jit(solution)/shard_map/place_blocks/pallas_call | solution.py:396
  (4 shorter events, 0.0 us)
Async XLA Ops:
  0.6 12.4 %collective-permute-start.1 = (bf16[512,256]{1,0:T(8,128)(2,1)}, bf16[512,256]{1,0:T(8,128)(2,1)S(1)}, u32[]{:S(2)}, u32[]{:S(2)}) collective-permute-start(bf16[512,256]{1,0:T(8,128)(2,1)} %refs_0_.1), channel_id=1, source_target_pairs={{0,4},{4,8},{8,12},{12,0},{1,5},{5,9},{9,13},{13,1},{2,6},{6,10},{... | collective-permute-start | bytes 786440 | tf_op jit(solution)/shard_map/ppermute | solution.py:328
  3.7 15.0 %collective-permute-start = (bf16[512,256]{1,0:T(8,128)(2,1)}, bf16[512,256]{1,0:T(8,128)(2,1)S(1)}, u32[]{:S(2)}, u32[]{:S(2)}) collective-permute-start(bf16[512,256]{1,0:T(8,128)(2,1)} %refs_1_.1), channel_id=1, source_target_pairs={{0,4},{4,8},{8,12},{12,0},{1,5},{5,9},{9,13},{13,1},{2,6},{6,10},{... | collective-permute-start | bytes 786440 | tf_op jit(solution)/shard_map/ppermute | solution.py:328
  13.1 15.3 %collective-permute-start.3 = (bf16[512,256]{1,0:T(8,128)(2,1)S(1)}, bf16[512,256]{1,0:T(8,128)(2,1)S(1)}, u32[]{:S(2)}, u32[]{:S(2)}) collective-permute-start(bf16[512,256]{1,0:T(8,128)(2,1)S(1)} %collective-permute-done.1.k_ref.refs_2_), channel_id=1, source_target_pairs={{0,4},{4,8},{8,12},{12,0},{1,5},{5,9},{9,13},{13,1},{2,6},{6,10},{... | collective-permute-start | bytes 786440 | tf_op jit(solution)/shard_map/ppermute | solution.py:355
  13.2 0.7 %copy-start.4 = (s32[4]{0:T(128)S(1)}, s32[4]{0:T(128)}, u32[]{:S(2)}) copy-start(s32[4]{0:T(128)} %lengths_ref.9) | copy-start | bytes 52
  13.9 1.2 %copy-start.6 = (bf16[512,1024]{1,0:T(8,128)(2,1)S(1)}, bf16[512,1024]{1,0:T(8,128)(2,1)}, u32[]{:S(2)}) copy-start(bf16[512,1024]{1,0:T(8,128)(2,1)} %q_ref.3) | copy-start | bytes 3145732
  15.1 0.9 %copy-start.8 = (f32[2,8,2048]{2,1,0:T(8,128)S(1)}, f32[2,8,2048]{2,1,0:T(8,128)}, u32[]{:S(2)}) copy-start(f32[2,8,2048]{2,1,0:T(8,128)} %get-tuple-element.19.old_top) | copy-start | bytes 393220
  16.0 9.1 %copy-start.9 = (bf16[8,16,512]{2,1,0:T(8,128)(2,1)S(1)}, bf16[8,16,512]{2,1,0:T(8,128)(2,1)}, u32[]{:S(2)}) copy-start(bf16[8,16,512]{2,1,0:T(8,128)(2,1)} %get-tuple-element.35) | copy-start | bytes 393220
  16.0 12.3 %copy-start.7 = (bf16[512,1024]{1,0:T(8,128)(2,1)S(1)}, bf16[512,1024]{1,0:T(8,128)(2,1)}, u32[]{:S(2)}) copy-start(bf16[512,1024]{1,0:T(8,128)(2,1)} %q_ref.3) | copy-start | bytes 3145732
  18.7 11.2 %collective-permute-start.2 = (bf16[512,256]{1,0:T(8,128)(2,1)S(1)}, bf16[512,256]{1,0:T(8,128)(2,1)S(1)}, u32[]{:S(2)}, u32[]{:S(2)}) collective-permute-start(bf16[512,256]{1,0:T(8,128)(2,1)S(1)} %collective-permute-done.v_ref.refs_3_), channel_id=1, source_target_pairs={{0,4},{4,8},{8,12},{12,0},{1,5},{5,9},{9,13},{13,1},{2,6},{6,10},{... | collective-permute-start | bytes 786440 | tf_op jit(solution)/shard_map/ppermute | solution.py:368
  20.8 1.6 %copy-start = (f32[2,128,2048]{2,1,0:T(8,128)S(1)}, f32[2,128,2048]{2,1,0:T(8,128)}, u32[]{:S(2)}) copy-start(f32[2,128,2048]{2,1,0:T(8,128)} %get-tuple-element.24.acc_in) | copy-start | bytes 6291460
  22.4 0.9 %copy-start.3 = (f32[2,8,2048]{2,1,0:T(8,128)S(1)}, f32[2,8,2048]{2,1,0:T(8,128)}, u32[]{:S(2)}) copy-start(f32[2,8,2048]{2,1,0:T(8,128)} %get-tuple-element.25.sum_in) | copy-start | bytes 393220
  25.2 6.7 %collective-permute-start.4 = (bf16[8,16,512]{2,1,0:T(8,128)(2,1)S(1)}, bf16[8,16,512]{2,1,0:T(8,128)(2,1)S(1)}, u32[]{:S(2)}, u32[]{:S(2)}) collective-permute-start(bf16[8,16,512]{2,1,0:T(8,128)(2,1)S(1)} %copy-done.9), channel_id=1, source_target_pairs={{0,12},{4,0},{8,4},{12,8},{1,13},{5,1},{9,5},{13,9},{2,14},{6,2},{... | collective-permute-start | bytes 393224 | tf_op jit(solution)/shard_map/ppermute | solution.py:390
  29.9 2.0 %copy-start.1 = (bf16[512,256]{1,0:T(8,128)(2,1)S(1)}, bf16[512,256]{1,0:T(8,128)(2,1)}, u32[]{:S(2)}) copy-start(bf16[512,256]{1,0:T(8,128)(2,1)} %refs_1_.1) | copy-start | bytes 786436
  29.9 2.0 %copy-start.2 = (bf16[512,256]{1,0:T(8,128)(2,1)S(1)}, bf16[512,256]{1,0:T(8,128)(2,1)}, u32[]{:S(2)}) copy-start(bf16[512,256]{1,0:T(8,128)(2,1)} %refs_0_.1) | copy-start | bytes 786436
  29.9 2.0 %copy-start.5 = (s32[128]{0:T(128)S(1)}, s32[128]{0:T(128)}, u32[]{:S(2)}) copy-start(s32[128]{0:T(128)} %slot_ref.3) | copy-start | bytes 1540
